TPU v7x, 32 devices: a whole 2x2x4 slice. The times are simulated.
32 devices in a mesh: blk: 8 (over y, x, core), wide: 4 (over z).
Axes of the slice: x: 2, y: 2, z: 4, core: 2. Of those that a mesh axis runs over, the one named last changes fastest.
Arguments:
- vectors: bfloat16 [16, 4096], P(None, ('blk', 'wide')), may hold values from -6 to 6
- blocks: bfloat16 [32, 4, 16, 128, 128], P(('blk', 'wide')), may hold values from -0.046875 to 0.046875
- columns: int32 [32, 4, 16], P(('blk', 'wide')), may hold values from 0 to 3
- counts: int32 [32, 4], P(('blk', 'wide')), may hold values from 1 to 16, as said below
Outputs:
- product: float32 [16, 4096], P(None, ('blk', 'wide'))
Inputs may be any that keep to these rules, and one draw needn't show every extreme that they name: `counts`: every block row has at least one live slot in every step; some block row fills all 16 slots of some step.
All inputs are finite; a program needn't handle non-finite values.
Results may differ from a plain program's by a relative error of at most 0.0003.
Values may be sent and summed in bfloat16 or wider, within the bound.
A program may use at most 64 MiB of HBM per device.

v0:
```python
import jax
import jax.numpy as jnp
from jax import lax
from jax.sharding import PartitionSpec as P


def passed_along(block, axis, distance):
    devices = range(lax.axis_size(axis))
    route = [((i - distance) % len(devices), i) for i in devices]
    return lax.ppermute(block, axis, route)


def shards(vectors, blocks, columns, counts):
    vec_count = vectors.shape[0]
    row_blocks = blocks.shape[0]
    half_steps = blocks.shape[1]
    slot_count = blocks.shape[2]
    block_size = blocks.shape[3]
    col_count = lax.axis_size("wide") * row_blocks
    own_rows = vectors.reshape(vec_count, row_blocks, block_size)
    live = (
        lax.broadcasted_iota(jnp.int32, (row_blocks, half_steps, slot_count), 2)
        < counts[:, :, None]
    )
    live_half = live.astype(jnp.bfloat16)
    live_full = live.astype(jnp.float32)
    select = (
        columns[:, :, :, None]
        == lax.broadcasted_iota(jnp.int32, (row_blocks, half_steps, slot_count, col_count), 3)
    ).astype(jnp.float32)
    direct_sum = jnp.zeros((vec_count, row_blocks, block_size), jnp.float32)
    panel = vectors
    carried = jnp.zeros((vec_count, row_blocks * block_size), jnp.float32)
    for step in range(half_steps):
        gathered = lax.all_gather(panel, "wide", axis=1, tiled=True)
        step_panel = gathered.reshape(vec_count, col_count, block_size)
        picked = jnp.take(step_panel, columns[:, step], axis=1)
        picked = picked * live_half[None, :, step, :, None]
        tiles = blocks[:, step]
        direct = jnp.einsum("rjic,krjc->kri", tiles, picked, preferred_element_type=jnp.float32)
        transposed = jnp.einsum(
            "rjic,kri->krjc", tiles, own_rows, preferred_element_type=jnp.float32
        )
        transposed = transposed * live_full[None, :, step, :, None]
        part = jnp.einsum(
            "krjc,rjn->knc", transposed, select[:, step], precision=lax.Precision.HIGHEST
        )
        direct, part = (direct, part.reshape(vec_count, col_count * block_size))
        direct_sum = direct_sum + direct
        carried = carried + lax.psum_scatter(part, "wide", scatter_dimension=1, tiled=True)
        if step + 1 < half_steps:
            panel = passed_along(panel, "blk", -1)
            carried = passed_along(carried, "blk", -1)
    share = passed_along(carried, "blk", half_steps - 1)
    return direct_sum.reshape(vec_count, row_blocks * block_size) + share


def solution(mesh):
    return jax.shard_map(
        shards,
        mesh=mesh,
        in_specs=(
            P(None, ("blk", "wide")),
            P(("blk", "wide"), None, None, None, None),
            P(("blk", "wide"), None, None),
            P(("blk", "wide"), None),
        ),
        out_specs=P(None, ("blk", "wide")),
        check_vma=False,
    )
```

profile of v0, /device:TPU:0, one launch (start us, length us, event | category | flops | bytes accessed | tf_op | source)
XLA Modules:
  0.0 101.4 jit_solution(6421066304271030389)
XLA Ops:
  6.5 3.4 %collective-permute-start = (bf16[16,128]{1,0:T(8,128)(2,1)}, bf16[16,128]{1,0:T(8,128)(2,1)S(1)}, u32[]{:S(2)}, u32[]{:S(2)}) collective-permute-start(bf16[16,128]{1,0:T(8,128)(2,1)} %param.6), channel_id=1, source_target_pairs={{4,0},{8,4},{12,8},{16,12},{20,16},{24,20},{28,24},{0,28},{5,1},{9... | collective-permute-start | bytes 12296 | tf_op jit(solution)/shard_map/ppermute | solution.py:10
  9.9 0.7 fusion.56
  10.7 0.7 iota_compare_fusion
  11.3 1.2 %convolution_multiply_fusion.3 = f32[16,16,128]{2,0,1:T(8,128)S(1)} fusion(bf16[1,4,16,128,128]{4,3,2,1,0:T(8,128)(2,1)} %param.7, f32[16]{0:T(128)S(1)} %get-tuple-element.17, bf16[16,128]{1,0:T(8,128)(2,1)} %param.6), kind=kOutput, calls=%fused_computation.7 | convolution fusion | flops 8421376 | bytes 659520 | tf_op jit(solution)/shard_map/rjic,kri->krjc/dot_general | solution.py:41
  12.6 0.2 fusion.25
  12.8 0.6 copy.40
  13.4 0.0 reduce-scatter.5.cloned.1.call-update
  13.4 0.0 reduce-scatter.7.cloned.1.call-start
  13.5 1.2 %convolution_multiply_fusion.2 = f32[16,16,128]{2,0,1:T(8,128)S(1)} fusion(bf16[1,4,16,128,128]{4,3,2,1,0:T(8,128)(2,1)} %param.7, f32[16]{0:T(128)S(1)} %get-tuple-element.16, bf16[16,128]{1,0:T(8,128)(2,1)} %param.6), kind=kOutput, calls=%fused_computation.6 | convolution fusion | flops 8421376 | bytes 659520 | tf_op jit(solution)/shard_map/rjic,kri->krjc/dot_general | solution.py:41
  14.7 0.2 fusion.23
  14.9 0.6 copy.39
  15.5 0.0 reduce-scatter.7.cloned.1.call-update
  15.6 0.0 reduce-scatter.9.cloned.1.call-start
  15.6 1.2 %convolution_multiply_fusion.1 = f32[16,16,128]{2,0,1:T(8,128)S(1)} fusion(bf16[1,4,16,128,128]{4,3,2,1,0:T(8,128)(2,1)} %param.7, f32[16]{0:T(128)S(1)} %get-tuple-element.15, bf16[16,128]{1,0:T(8,128)(2,1)} %param.6), kind=kOutput, calls=%fused_computation.5 | convolution fusion | flops 8421376 | bytes 659520 | tf_op jit(solution)/shard_map/rjic,kri->krjc/dot_general | solution.py:41
  16.8 0.2 fusion.21
  17.1 0.6 copy.38
  17.7 0.0 reduce-scatter.9.cloned.1.call-update
  17.7 0.0 reduce-scatter.11.cloned.1.call-start
  17.8 0.2 convolution_multiply_fusion
  17.9 0.2 fusion.19
  18.1 0.6 copy.37
  18.8 0.0 reduce-scatter.11.cloned.1.call-update
  18.8 12.1 %all_gather.12 = bf16[16,512]{1,0:T(8,128)(2,1)S(1)} all-gather(bf16[16,128]{1,0:T(8,128)(2,1)S(1)} %copy-done.1), channel_id=1, replica_groups=mesh['blk'=8,'wide'=4] {'wide'}, dimensions={1}, use_global_device_ids=true | all-gather | bytes 20480 | tf_op jit(solution)/shard_map/all_gather | solution.py:35
  31.0 0.6 gather_fusion
  31.6 0.3 convolution_bitcast_fusion.3
  31.9 11.9 %all_gather.13 = bf16[16,512]{1,0:T(8,128)(2,1)S(1)} all-gather(bf16[16,128]{1,0:T(8,128)(2,1)S(1)} %collective-permute-done), channel_id=1, replica_groups=mesh['blk'=8,'wide'=4] {'wide'}, dimensions={1}, use_global_device_ids=true | all-gather | bytes 20480 | tf_op jit(solution)/shard_map/all_gather | solution.py:35
  43.7 0.6 gather_fusion.1
  44.3 0.1 collective-permute-start.1
  44.4 0.0 reduce-scatter.5.cloned.1.call-done
  44.4 0.8 collective-permute-start.3
  45.2 0.3 fusion.2
  45.5 0.2 collective-permute-done.1
  45.7 11.9 %all_gather.14 = bf16[16,512]{1,0:T(8,128)(2,1)S(1)} all-gather(bf16[16,128]{1,0:T(8,128)(2,1)S(1)} %collective-permute-done.1), channel_id=1, replica_groups=mesh['blk'=8,'wide'=4] {'wide'}, dimensions={1}, use_global_device_ids=true | all-gather | bytes 20480 | tf_op jit(solution)/shard_map/all_gather | solution.py:35
  57.6 0.0 collective-permute-done.3
  57.6 0.7 add.38
  58.3 0.0 collective-permute-start.4
  58.3 0.6 gather_fusion.2
  58.9 1.2 %collective-permute-start.2 = (bf16[16,128]{1,0:T(8,128)(2,1)S(1)}, bf16[16,128]{1,0:T(8,128)(2,1)S(1)}, u32[]{:S(2)}, u32[]{:S(2)}) collective-permute-start(bf16[16,128]{1,0:T(8,128)(2,1)S(1)} %collective-permute-done.1), channel_id=1, source_target_pairs={{4,0},{8,4},{12,8},{16,12},{20,16},{24,20},{28,24},{0,28},{5,1},{9... | collective-permute-start | bytes 12296 | tf_op jit(solution)/shard_map/ppermute | solution.py:10
  60.1 10.8 %reduce-scatter.9.cloned.1.call-done = f32[16,128]{1,0:T(8,128)} async-done(((f32[16,512]{1,0:T(8,128)}), f32[16,128]{1,0:T(8,128)}) %reduce-scatter.9.cloned.1.call-update) | async-done | bytes 8208 | tf_op jit(solution)/shard_map/reduce_scatter | solution.py:50
  70.9 0.0 collective-permute-done.4
  70.9 0.7 add.39
  71.6 0.3 fusion.1
  71.9 11.9 %all_gather.15 = bf16[16,512]{1,0:T(8,128)(2,1)S(1)} all-gather(bf16[16,128]{1,0:T(8,128)(2,1)S(1)} %collective-permute-done.2), channel_id=1, replica_groups=mesh['blk'=8,'wide'=4] {'wide'}, dimensions={1}, use_global_device_ids=true | all-gather | bytes 20480 | tf_op jit(solution)/shard_map/all_gather | solution.py:35
  83.8 6.4 %reduce-scatter.11.cloned.1.call-done = f32[16,128]{1,0:T(8,128)} async-done(((f32[16,512]{1,0:T(8,128)}), f32[16,128]{1,0:T(8,128)}) %reduce-scatter.11.cloned.1.call-update) | async-done | bytes 8208 | tf_op jit(solution)/shard_map/reduce_scatter | solution.py:50
  90.2 0.7 add.40
  90.9 0.6 gather_fusion.3
  91.5 2.5 %collective-permute-done.6 = f32[16,128]{1,0:T(8,128)S(1)} collective-permute-done((f32[16,128]{1,0:T(8,128)S(1)}, f32[16,128]{1,0:T(8,128)S(1)}, u32[]{:S(2)}, u32[]{:S(2)}) %collective-permute-start.6) | collective-permute-done | bytes 8224 | tf_op jit(solution)/shard_map/ppermute | solution.py:10
  94.0 0.9 fusion.61
  (25 shorter events, 0.1 us)
Async XLA Ops:
  6.5 11.2 %copy-start.1 = (bf16[16,128]{1,0:T(8,128)(2,1)S(1)}, bf16[16,128]{1,0:T(8,128)(2,1)}, u32[]{:S(2)}) copy-start(bf16[16,128]{1,0:T(8,128)(2,1)} %param.6) | copy-start | bytes 12292
  6.5 24.4 %copy-start.2 = (s32[1,4,16]{2,1,0:T(4,128)S(1)}, s32[1,4,16]{2,1,0:T(4,128)}, u32[]{:S(2)}) copy-start(s32[1,4,16]{2,1,0:T(4,128)} %param.8) | copy-start | bytes 772
  6.5 11.2 %copy-start = (bf16[1,4,16,128,128]{4,3,2,1,0:T(8,128)(2,1)S(1)}, bf16[1,4,16,128,128]{4,3,2,1,0:T(8,128)(2,1)}, u32[]{:S(2)}) copy-start(bf16[1,4,16,128,128]{4,3,2,1,0:T(8,128)(2,1)} %param.7) | copy-start | bytes 6291460
  6.5 37.9 %reduce-scatter.5.cloned.1.call-start = ((), (), s32[]{:S(2)}) async-start(), calls=%async_computation.4 | async-start | bytes 40960 | tf_op jit(solution)/shard_map/reduce_scatter | solution.py:50
  6.5 25.3 %collective-permute-start = (bf16[16,128]{1,0:T(8,128)(2,1)}, bf16[16,128]{1,0:T(8,128)(2,1)S(1)}, u32[]{:S(2)}, u32[]{:S(2)}) collective-permute-start(bf16[16,128]{1,0:T(8,128)(2,1)} %param.6), channel_id=1, source_target_pairs={{4,0},{8,4},{12,8},{16,12},{20,16},{24,20},{28,24},{0,28},{5,1},{9... | collective-permute-start | bytes 12296 | tf_op jit(solution)/shard_map/ppermute | solution.py:10
  13.4 44.1 %reduce-scatter.7.cloned.1.call-start = ((), (), s32[]{:S(2)}) async-start(), calls=%async_computation.5 | async-start | bytes 40960 | tf_op jit(solution)/shard_map/reduce_scatter | solution.py:50
  15.6 55.3 %reduce-scatter.9.cloned.1.call-start = ((), (), s32[]{:S(2)}) async-start(), calls=%async_computation.6 | async-start | bytes 40960 | tf_op jit(solution)/shard_map/reduce_scatter | solution.py:50
  17.7 72.5 %reduce-scatter.11.cloned.1.call-start = ((), (), s32[]{:S(2)}) async-start(), calls=%async_computation.7 | async-start | bytes 40960 | tf_op jit(solution)/shard_map/reduce_scatter | solution.py:50
  44.3 1.4 %collective-permute-start.1 = (bf16[16,128]{1,0:T(8,128)(2,1)S(1)}, bf16[16,128]{1,0:T(8,128)(2,1)S(1)}, u32[]{:S(2)}, u32[]{:S(2)}) collective-permute-start(bf16[16,128]{1,0:T(8,128)(2,1)S(1)} %collective-permute-done), channel_id=1, source_target_pairs={{4,0},{8,4},{12,8},{16,12},{20,16},{24,20},{28,24},{0,28},{5,1},{9... | collective-permute-start | bytes 12296 | tf_op jit(solution)/shard_map/ppermute | solution.py:10
  44.4 13.2 %collective-permute-start.3 = (f32[16,128]{1,0:T(8,128)}, f32[16,128]{1,0:T(8,128)S(1)}, u32[]{:S(2)}, u32[]{:S(2)}) collective-permute-start(f32[16,128]{1,0:T(8,128)} %reduce-scatter.5.cloned.1.call-done), channel_id=1, source_target_pairs={{4,0},{8,4},{12,8},{16,12},{20,16},{24,20},{28,24},{0,28},{5,1},{9... | collective-permute-start | bytes 24584 | tf_op jit(solution)/shard_map/ppermute | solution.py:10
  58.3 12.6 %collective-permute-start.4 = (f32[16,128]{1,0:T(8,128)S(1)}, f32[16,128]{1,0:T(8,128)S(1)}, u32[]{:S(2)}, u32[]{:S(2)}) collective-permute-start(f32[16,128]{1,0:T(8,128)S(1)} %add.38), channel_id=1, source_target_pairs={{4,0},{8,4},{12,8},{16,12},{20,16},{24,20},{28,24},{0,28},{5,1},{9... | collective-permute-start | bytes 24584 | tf_op jit(solution)/shard_map/ppermute | solution.py:10
  58.9 13.0 %collective-permute-start.2 = (bf16[16,128]{1,0:T(8,128)(2,1)S(1)}, bf16[16,128]{1,0:T(8,128)(2,1)S(1)}, u32[]{:S(2)}, u32[]{:S(2)}) collective-permute-start(bf16[16,128]{1,0:T(8,128)(2,1)S(1)} %collective-permute-done.1), channel_id=1, source_target_pairs={{4,0},{8,4},{12,8},{16,12},{20,16},{24,20},{28,24},{0,28},{5,1},{9... | collective-permute-start | bytes 12296 | tf_op jit(solution)/shard_map/ppermute | solution.py:10
  71.6 18.6 %collective-permute-start.5 = (f32[16,128]{1,0:T(8,128)S(1)}, f32[16,128]{1,0:T(8,128)S(1)}, u32[]{:S(2)}, u32[]{:S(2)}) collective-permute-start(f32[16,128]{1,0:T(8,128)S(1)} %add.39), channel_id=1, source_target_pairs={{4,0},{8,4},{12,8},{16,12},{20,16},{24,20},{28,24},{0,28},{5,1},{9... | collective-permute-start | bytes 24584 | tf_op jit(solution)/shard_map/ppermute | solution.py:10
  90.9 3.1 %collective-permute-start.6 = (f32[16,128]{1,0:T(8,128)S(1)}, f32[16,128]{1,0:T(8,128)S(1)}, u32[]{:S(2)}, u32[]{:S(2)}) collective-permute-start(f32[16,128]{1,0:T(8,128)S(1)} %add.40), channel_id=1, source_target_pairs={{20,0},{24,4},{28,8},{0,12},{4,16},{8,20},{12,24},{16,28},{21,1},{... | collective-permute-start | bytes 24584 | tf_op jit(solution)/shard_map/ppermute | solution.py:10
Sparse Core Ops, SparseCore 0:
  13.5 18.5 reduce-scatter.4
  34.4 17.0 reduce-scatter.6
  53.8 17.0 reduce-scatter.8
  73.1 17.0 reduce-scatter.10
where the time goes:
time: 102 us; the launch traced here: 101 us
  blocking collectives  47.7 us (47%)
  waiting for transfers between devices  20 us (20%)
  between operations  13.3 us (13%)
  matrix products  6.39 us (6%)
  starting transfers between devices  5.61 us (6%)
  local copies, waits for them, and re-layouts  4.79 us (5%)
  other arithmetic  3.57 us (4%)
    all_gather x4, blocking collectives, shards(): gathered = lax.all_gather(panel, 'wide', axis=1, tiled=True)  47.7 us
    reduce_scatter x4, waiting for transfers between devices, shards(): lax.psum_scatter(part, 'wide', scatter_dimension=1, tiled=True)  17.3 us
    ppermute x7, starting transfers between devices, passed_along(): return lax.ppermute(block, axis, route)  5.48 us
    dot_general x4, matrix products, shards(): jnp.einsum('rjic,kri->krjc', tiles, own_rows, preferred_element_type=jnp....  3.8 us
    ppermute x7, waiting for transfers between devices, passed_along(): return lax.ppermute(block, axis, route)  2.7 us
    unnamed x10, local copies, waits for them, and re-layouts  2.47 us
    gather x4, local copies, waits for them, and re-layouts, shards(): picked = jnp.take(step_panel, columns[:, step], axis=1)  2.29 us
    add x3, other arithmetic, shards(): carried + lax.psum_scatter(part, 'wide', scatter_dimension=1, tiled=True)  2.1 us
  transfers between devices with their start and end apart: 11, of which 4 were waited for; matrix products, arithmetic and copies ran while one was open for 13% of the time, Pallas kernels for 0%

commit v1 on v0

v1 whole, which is shorter than its diff:
```python
import functools

import jax
import jax.numpy as jnp
from jax import lax
from jax.experimental import pallas as pl
from jax.experimental.pallas import tpu as pltpu
from jax.sharding import PartitionSpec as P

MESH = pl.DeviceIdType.MESH


def kernel(groups, wide, steps, cols, counts, vec, blocks, out, *scratch):
    panels = scratch[:steps]
    tiles = scratch[steps : 2 * steps]
    (parts, landed, total, shares, load_sem, a_send, a_recv, b_send, b_recv,
     p_send, p_recv, z_send, z_recv) = scratch[2 * steps :]
    slots = blocks.shape[2]
    size = blocks.shape[3]
    vecs = vec.shape[0]
    g = lax.axis_index("blk")
    w = lax.axis_index("wide")

    def group(offset):
        return (lax.rem(g + (offset + groups), groups), w)

    def owner(offset):
        return (g, lax.rem(w + offset, wide))

    order = [*range(1, steps), 0]
    loads = {}
    for s in order:
        loads[s] = pltpu.make_async_copy(blocks.at[0, s], tiles[s], load_sem.at[s])
        loads[s].start()

    barrier = pltpu.get_barrier_semaphore()
    peers = [owner(d) for d in range(1, wide)]
    for d in range(1, steps):
        peers += [group(d), group(-d)]
    for peer in peers:
        pl.semaphore_signal(barrier, inc=1, device_id=peer, device_id_type=MESH)
    panels[0][w] = vec[...]
    pl.semaphore_wait(barrier, len(peers))

    def remote(src, dst, send, recv, to):
        return pltpu.make_async_remote_copy(
            src_ref=src, dst_ref=dst, send_sem=send, recv_sem=recv, device_id=to, device_id_type=MESH
        )

    spread = [
        remote(vec, panels[0].at[w], a_send.at[d - 1], a_recv.at[d - 1], owner(d))
        for d in range(1, wide)
    ]
    for c in spread:
        c.start()

    own = vec[...]
    none = jnp.zeros_like(own)

    def live(s, j):
        return j < counts[0, s]

    def transposed(s):
        loads[s].wait()
        left = []
        for j in range(slots):
            code = jnp.where(live(s, j), cols[0, s, j], -1)
            left.append(
                jnp.concatenate([jnp.where(code == n, own, none) for n in range(wide)], axis=0)
            )
        left = jnp.concatenate(left, axis=1)
        part = jnp.dot(
            left, tiles[s][...].reshape(slots * size, size), preferred_element_type=jnp.float32
        )
        parts[s] = part.reshape(wide, vecs, size)

    def direct(s):
        left = [jnp.where(live(s, j), panels[s][cols[0, s, j]], none) for j in range(slots)]
        left = jnp.concatenate(left, axis=1)
        right = jnp.concatenate([tiles[s][j] for j in range(slots)], axis=1)
        return lax.dot_general(
            left, right, (((1,), (1,)), ((), ())), preferred_element_type=jnp.float32
        )

    passed, handed = [], []
    for s in order:
        transposed(s)
        if s:
            c = remote(parts.at[s], landed.at[s - 1], p_send.at[s - 1], p_recv.at[s - 1], group(s))
            c.start()
            handed.append(c)
        if s == 1:
            for c in spread:
                c.wait_recv()
            for d in range(1, steps):
                c = remote(panels[0], panels[d], b_send.at[d - 1], b_recv.at[d - 1], group(-d))
                c.start()
                passed.append(c)

    answer = direct(0)
    for s in range(1, steps):
        passed[s - 1].wait_recv()
        answer += direct(s)

    summed = parts[0]
    for s in range(1, steps):
        handed[s - 1].wait_recv()
        summed += landed[s - 1]
    total[...] = summed
    returned = []
    for d in range(1, wide):
        to = owner(d)
        c = remote(total.at[to[1]], shares.at[d - 1], z_send.at[d - 1], z_recv.at[d - 1], to)
        c.start()
        returned.append(c)
    answer += total[w]
    for d in range(1, wide):
        returned[d - 1].wait_recv()
        answer += shares[d - 1]
    out[...] = answer
    for c in (*spread, *passed, *handed, *returned):
        c.wait_send()


def shards(mesh, vectors, blocks, columns, counts):
    groups, wide = mesh.shape["blk"], mesh.shape["wide"]
    vecs, size = vectors.shape
    _, steps, slots = blocks.shape[:3]
    sems = pltpu.SemaphoreType.DMA
    return pl.pallas_call(
        functools.partial(kernel, groups, wide, steps),
        out_shape=jax.ShapeDtypeStruct((vecs, size), jnp.float32),
        in_specs=[
            pl.BlockSpec(memory_space=pltpu.SMEM),
            pl.BlockSpec(memory_space=pltpu.SMEM),
            pl.BlockSpec(memory_space=pltpu.VMEM),
            pl.BlockSpec(memory_space=pl.ANY),
        ],
        out_specs=pl.BlockSpec(memory_space=pltpu.VMEM),
        scratch_shapes=[
            *[pltpu.VMEM((wide, vecs, size), jnp.bfloat16)] * steps,
            *[pltpu.VMEM((slots, size, size), jnp.bfloat16)] * steps,
            pltpu.VMEM((steps, wide, vecs, size), jnp.float32),
            pltpu.VMEM((steps - 1, wide, vecs, size), jnp.float32),
            pltpu.VMEM((wide, vecs, size), jnp.float32),
            pltpu.VMEM((wide - 1, vecs, size), jnp.float32),
            sems((steps,)),
            sems((wide - 1,)),
            sems((wide - 1,)),
            sems((steps - 1,)),
            sems((steps - 1,)),
            sems((steps - 1,)),
            sems((steps - 1,)),
            sems((wide - 1,)),
            sems((wide - 1,)),
        ],
        compiler_params=pltpu.CompilerParams(
            collective_id=0, has_side_effects=True, vmem_limit_bytes=14 << 20
        ),
    )(columns, counts, vectors, blocks)


def solution(mesh):
    return jax.shard_map(
        functools.partial(shards, mesh),
        mesh=mesh,
        in_specs=(
            P(None, ("blk", "wide")),
            P(("blk", "wide"), None, None, None, None),
            P(("blk", "wide"), None, None),
            P(("blk", "wide"), None),
        ),
        out_specs=P(None, ("blk", "wide")),
        check_vma=False,
    )
```

time: 102 us -> 22.3 us (0.22)
  blocking collectives: 47.7 us -> 0 us
  waiting for transfers between devices: 20 us -> 0 us
  Pallas kernels: 0 us -> 17.9 us
  between operations: 13.3 us -> 0.01 us
  matrix products: 6.39 us -> 0 us
  starting transfers between devices: 5.61 us -> 0 us
  other arithmetic: 3.57 us -> 0 us
    all_gather x4 -> x0, blocking collectives: 47.7 us -> none  [shards(): gathered = lax.all_gather(panel, 'wide', axis=1, tiled=True)]
    pallas_call x0 -> x1, Pallas kernels: none -> 17.9 us  [shards(): pl.pallas_call(functools.partial(kernel, groups, wide, steps), out_shape=...]
    reduce_scatter x4 -> x0, waiting for transfers between devices: 17.3 us -> none  [shards(): lax.psum_scatter(part, 'wide', scatter_dimension=1, tiled=True)]
    dot_general x12 -> x0, matrix products: 6.39 us -> none  [the longest x4 3.8 us: shards(): jnp.einsum('rjic,kri->krjc', tiles, own_rows, preferred_element_type=jnp....]
    ppermute x7 -> x0, starting transfers between devices: 5.48 us -> none  [passed_along(): return lax.ppermute(block, axis, route)]
    ppermute x7 -> x0, waiting for transfers between devices: 2.7 us -> none  [passed_along(): return lax.ppermute(block, axis, route)]
    gather x4 -> x0, local copies, waits for them, and re-layouts: 2.29 us -> none  [shards(): picked = jnp.take(step_panel, columns[:, step], axis=1)]
    add x3 -> x0, other arithmetic: 2.1 us -> none  [shards(): carried + lax.psum_scatter(part, 'wide', scatter_dimension=1, tiled=True)]
  transfers between devices with their start and end apart: 11 -> 0, of which waited for: 4 -> 0; matrix products, arithmetic and copies ran while one was open for 13% -> 0% of each run, Pallas kernels for 0% -> 0%
where the time goes in v1:
time: 22.3 us; the launch traced here: 22.1 us
  Pallas kernels  17.9 us (80%)
  local copies, waits for them, and re-layouts  4.21 us (19%)
    pallas_call x1, Pallas kernels, shards(): pl.pallas_call(functools.partial(kernel, groups, wide, steps), out_shape=...  17.9 us
    unnamed x9, local copies, waits for them, and re-layouts  4.21 us

profile of v1, /device:TPU:0, one launch (start us, length us, event | category | flops | bytes accessed | tf_op | source)
XLA Modules:
  0.0 22.1 jit_solution(3911350235442203043)
XLA Ops:
  0.0 0.0 copy-start
  0.0 1.6 %copy-done = bf16[1,4,16,128,128]{4,3,2,1,0:T(8,128)(2,1)S(1)} copy-done((bf16[1,4,16,128,128]{4,3,2,1,0:T(8,128)(2,1)S(1)}, bf16[1,4,16,128,128]{4,3,2,1,0:T(8,128)(2,1)}, u32[]{:S(2)}) %copy-start) | copy-done | bytes 2097176
  1.6 0.0 copy-start.1
  1.6 0.7 %copy-done.1 = bf16[16,128]{1,0:T(8,128)(2,1)S(1)} copy-done((bf16[16,128]{1,0:T(8,128)(2,1)S(1)}, bf16[16,128]{1,0:T(8,128)(2,1)}, u32[]{:S(2)}) %copy-start.1) | copy-done | bytes 4120
  2.3 0.0 copy-start.2
  2.3 0.7 %copy-done.2 = s32[1,4,16]{2,1,0:T(4,128)S(1)} copy-done((s32[1,4,16]{2,1,0:T(4,128)S(1)}, s32[1,4,16]{2,1,0:T(4,128)}, u32[]{:S(2)}) %copy-start.2) | copy-done | bytes 280
  3.0 0.0 copy-start.3
  3.0 0.7 %copy-done.3 = s32[1,4]{1,0:T(1,128)S(1)} copy-done((s32[1,4]{1,0:T(1,128)S(1)}, s32[1,4]{1,0:T(1,128)}, u32[]{:S(2)}) %copy-start.3) | copy-done | bytes 40
  3.6 17.9 %shard_map.46 = f32[16,128]{1,0:T(8,128)S(1)} custom-call(s32[1,4,16]{2,1,0:T(4,128)S(1)} %copy-done.2, s32[1,4]{1,0:T(1,128)S(1)} %copy-done.3, bf16[16,128]{1,0:T(8,128)(2,1)S(1)} %copy-done.1, bf16[1,4,16,128,128]{4,3,2,1,0:T(8,128)(2,1)S(1)} %copy-done), custom_call_target="tpu_custom_call" | custom-call | tf_op jit(solution)/shard_map/pallas_call | solution.py:130
  21.5 0.6 %copy.6 = f32[16,128]{1,0:T(8,128)} copy(f32[16,128]{1,0:T(8,128)S(1)} %shard_map.46) | data formatting | bytes 16384
Async XLA Ops:
  0.0 1.6 %copy-start = (bf16[1,4,16,128,128]{4,3,2,1,0:T(8,128)(2,1)S(1)}, bf16[1,4,16,128,128]{4,3,2,1,0:T(8,128)(2,1)}, u32[]{:S(2)}) copy-start(bf16[1,4,16,128,128]{4,3,2,1,0:T(8,128)(2,1)} %blocks.1) | copy-start | bytes 6291460
  1.6 0.7 %copy-start.1 = (bf16[16,128]{1,0:T(8,128)(2,1)S(1)}, bf16[16,128]{1,0:T(8,128)(2,1)}, u32[]{:S(2)}) copy-start(bf16[16,128]{1,0:T(8,128)(2,1)} %vec.1) | copy-start | bytes 12292
  2.3 0.7 %copy-start.2 = (s32[1,4,16]{2,1,0:T(4,128)S(1)}, s32[1,4,16]{2,1,0:T(4,128)}, u32[]{:S(2)}) copy-start(s32[1,4,16]{2,1,0:T(4,128)} %cols.1) | copy-start | bytes 772
  3.0 0.7 %copy-start.3 = (s32[1,4]{1,0:T(1,128)S(1)}, s32[1,4]{1,0:T(1,128)}, u32[]{:S(2)}) copy-start(s32[1,4]{1,0:T(1,128)} %counts.1) | copy-start | bytes 52

commit v2 on v1

--- a/solution.py
+++ b/solution.py
@@ -10,14 +10,14 @@
 MESH = pl.DeviceIdType.MESH
 
 
-def kernel(groups, wide, steps, cols, counts, vec, blocks, out, *scratch):
+def kernel(groups, wide, steps, cols_in, counts_in, vec_in, blocks, out, *scratch):
     panels = scratch[:steps]
     tiles = scratch[steps : 2 * steps]
-    (parts, landed, total, shares, load_sem, a_send, a_recv, b_send, b_recv,
+    (cols, counts, vec, parts, landed, total, shares, in_sem, load_sem, a_send, a_recv, b_send, b_recv,
      p_send, p_recv, z_send, z_recv) = scratch[2 * steps :]
     slots = blocks.shape[2]
     size = blocks.shape[3]
-    vecs = vec.shape[0]
+    vecs = vec_in.shape[0]
     g = lax.axis_index("blk")
     w = lax.axis_index("wide")
 
@@ -27,6 +27,12 @@
     def owner(offset):
         return (g, lax.rem(w + offset, wide))
 
+    small = [
+        pltpu.make_async_copy(src, dst, in_sem.at[i])
+        for i, (src, dst) in enumerate(((vec_in, vec), (cols_in, cols), (counts_in, counts)))
+    ]
+    for c in small:
+        c.start()
     order = [*range(1, steps), 0]
     loads = {}
     for s in order:
@@ -39,6 +45,7 @@
         peers += [group(d), group(-d)]
     for peer in peers:
         pl.semaphore_signal(barrier, inc=1, device_id=peer, device_id_type=MESH)
+    small[0].wait()
     panels[0][w] = vec[...]
     pl.semaphore_wait(barrier, len(peers))
 
@@ -54,6 +61,8 @@
     for c in spread:
         c.start()
 
+    for c in small[1:]:
+        c.wait()
     own = vec[...]
     none = jnp.zeros_like(own)
 
@@ -130,20 +139,19 @@
     return pl.pallas_call(
         functools.partial(kernel, groups, wide, steps),
         out_shape=jax.ShapeDtypeStruct((vecs, size), jnp.float32),
-        in_specs=[
-            pl.BlockSpec(memory_space=pltpu.SMEM),
-            pl.BlockSpec(memory_space=pltpu.SMEM),
-            pl.BlockSpec(memory_space=pltpu.VMEM),
-            pl.BlockSpec(memory_space=pl.ANY),
-        ],
+        in_specs=[pl.BlockSpec(memory_space=pltpu.HBM)] * 4,
         out_specs=pl.BlockSpec(memory_space=pltpu.VMEM),
         scratch_shapes=[
             *[pltpu.VMEM((wide, vecs, size), jnp.bfloat16)] * steps,
             *[pltpu.VMEM((slots, size, size), jnp.bfloat16)] * steps,
+            pltpu.SMEM(columns.shape, jnp.int32),
+            pltpu.SMEM(counts.shape, jnp.int32),
+            pltpu.VMEM((vecs, size), jnp.bfloat16),
             pltpu.VMEM((steps, wide, vecs, size), jnp.float32),
             pltpu.VMEM((steps - 1, wide, vecs, size), jnp.float32),
             pltpu.VMEM((wide, vecs, size), jnp.float32),
             pltpu.VMEM((wide - 1, vecs, size), jnp.float32),
+            sems((3,)),
             sems((steps,)),
             sems((wide - 1,)),
             sems((wide - 1,)),
@@ -155,7 +163,7 @@
             sems((wide - 1,)),
         ],
         compiler_params=pltpu.CompilerParams(
-            collective_id=0, has_side_effects=True, vmem_limit_bytes=14 << 20
+            collective_id=0, has_side_effects=True, vmem_limit_bytes=60 << 20
         ),
     )(columns, counts, vectors, blocks)
 

time: 22.3 us -> 19.3 us (0.87)
  local copies, waits for them, and re-layouts: 4.21 us -> 1.3 us
    unnamed x9 -> x1, local copies, waits for them, and re-layouts: 4.21 us -> 1.3 us
where the time goes in v2:
time: 19.3 us; the launch traced here: 19.1 us
  Pallas kernels  17.8 us (92%)
  local copies, waits for them, and re-layouts  1.3 us (7%)
    pallas_call x1, Pallas kernels, shards(): pl.pallas_call(functools.partial(kernel, groups, wide, steps), out_shape=...  17.8 us
    unnamed x1, local copies, waits for them, and re-layouts  1.3 us

profile of v2, /device:TPU:0, one launch (start us, length us, event | category | flops | bytes accessed | tf_op | source)
XLA Modules:
  0.0 19.1 jit_solution(14859048761005202026)
XLA Ops:
  0.0 17.8 %shard_map.46 = f32[16,128]{1,0:T(8,128)} custom-call(s32[1,4,16]{2,1,0:T(4,128)} %cols_in.1, s32[1,4]{1,0:T(1,128)} %counts_in.1, bf16[16,128]{1,0:T(8,128)(2,1)} %vec_in.1, bf16[1,4,16,128,128]{4,3,2,1,0:T(8,128)(2,1)} %blocks.1), custom_call_target="tpu_custom_call" | custom-call | tf_op jit(solution)/shard_map/pallas_call | solution.py:139
  17.8 1.3 %copy.6 = f32[16,128]{1,0:T(8,128)} copy(f32[16,128]{1,0:T(8,128)} %shard_map.46) | data formatting | bytes 16384

commit v3 on v2

--- a/solution.py
+++ b/solution.py
@@ -98,19 +98,15 @@
             c = remote(parts.at[s], landed.at[s - 1], p_send.at[s - 1], p_recv.at[s - 1], group(s))
             c.start()
             handed.append(c)
-        if s == 1:
-            for c in spread:
-                c.wait_recv()
-            for d in range(1, steps):
-                c = remote(panels[0], panels[d], b_send.at[d - 1], b_recv.at[d - 1], group(-d))
-                c.start()
-                passed.append(c)
+
+    for c in spread:
+        c.wait_recv()
+    for d in range(1, steps):
+        c = remote(panels[0], panels[d], b_send.at[d - 1], b_recv.at[d - 1], group(-d))
+        c.start()
+        passed.append(c)
 
     answer = direct(0)
-    for s in range(1, steps):
-        passed[s - 1].wait_recv()
-        answer += direct(s)
-
     summed = parts[0]
     for s in range(1, steps):
         handed[s - 1].wait_recv()
@@ -123,6 +119,9 @@
         c.start()
         returned.append(c)
     answer += total[w]
+    for s in range(1, steps):
+        passed[s - 1].wait_recv()
+        answer += direct(s)
     for d in range(1, wide):
         returned[d - 1].wait_recv()
         answer += shares[d - 1]

time: 19.3 us -> 14.9 us (0.77)
  Pallas kernels: 17.8 us -> 13.4 us
    pallas_call x1, Pallas kernels: 17.8 us -> 13.4 us  [shards(): pl.pallas_call(functools.partial(kernel, groups, wide, steps), out_shape=...]
where the time goes in v3:
time: 14.9 us; the launch traced here: 14.7 us
  Pallas kernels  13.4 us (90%)
  local copies, waits for them, and re-layouts  1.3 us (9%)
    pallas_call x1, Pallas kernels, shards(): pl.pallas_call(functools.partial(kernel, groups, wide, steps), out_shape=...  13.4 us
    unnamed x1, local copies, waits for them, and re-layouts  1.3 us

profile of v3, /device:TPU:0, one launch (start us, length us, event | category | flops | bytes accessed | tf_op | source)
XLA Modules:
  0.0 14.7 jit_solution(14977247521072992423)
XLA Ops:
  0.0 13.4 %shard_map.46 = f32[16,128]{1,0:T(8,128)} custom-call(s32[1,4,16]{2,1,0:T(4,128)} %cols_in.1, s32[1,4]{1,0:T(1,128)} %counts_in.1, bf16[16,128]{1,0:T(8,128)(2,1)} %vec_in.1, bf16[1,4,16,128,128]{4,3,2,1,0:T(8,128)(2,1)} %blocks.1), custom_call_target="tpu_custom_call" | custom-call | tf_op jit(solution)/shard_map/pallas_call | solution.py:138
  13.4 1.3 %copy.6 = f32[16,128]{1,0:T(8,128)} copy(f32[16,128]{1,0:T(8,128)} %shard_map.46) | data formatting | bytes 16384

commit v4 on v3

--- a/solution.py
+++ b/solution.py
@@ -106,7 +106,6 @@
         c.start()
         passed.append(c)
 
-    answer = direct(0)
     summed = parts[0]
     for s in range(1, steps):
         handed[s - 1].wait_recv()
@@ -118,7 +117,7 @@
         c = remote(total.at[to[1]], shares.at[d - 1], z_send.at[d - 1], z_recv.at[d - 1], to)
         c.start()
         returned.append(c)
-    answer += total[w]
+    answer = direct(0) + total[w]
     for s in range(1, steps):
         passed[s - 1].wait_recv()
         answer += direct(s)
@@ -137,7 +136,7 @@
     sems = pltpu.SemaphoreType.DMA
     return pl.pallas_call(
         functools.partial(kernel, groups, wide, steps),
-        out_shape=jax.ShapeDtypeStruct((vecs, size), jnp.float32),
+        out_shape=pltpu.VMEM((vecs, size), jnp.float32),
         in_specs=[pl.BlockSpec(memory_space=pltpu.HBM)] * 4,
         out_specs=pl.BlockSpec(memory_space=pltpu.VMEM),
         scratch_shapes=[

time: 14.9 us -> 13.6 us (0.913)
  local copies, waits for them, and re-layouts: 1.3 us -> 0.6 us
  Pallas kernels: 13.4 us -> 12.8 us
    unnamed x1, local copies, waits for them, and re-layouts: 1.3 us -> 0.6 us
    pallas_call x1, Pallas kernels: 13.4 us -> 12.8 us  [shards(): pl.pallas_call(functools.partial(kernel, groups, wide, steps), out_shape=...]
where the time goes in v4:
time: 13.6 us; the launch traced here: 13.4 us
  Pallas kernels  12.8 us (94%)
  local copies, waits for them, and re-layouts  0.6 us (4%)
    pallas_call x1, Pallas kernels, shards(): pl.pallas_call(functools.partial(kernel, groups, wide, steps), out_shape=...  12.8 us
    unnamed x1, local copies, waits for them, and re-layouts  0.6 us

profile of v4, /device:TPU:0, one launch (start us, length us, event | category | flops | bytes accessed | tf_op | source)
XLA Modules:
  0.0 13.4 jit_solution(9020149655224895400)
XLA Ops:
  0.0 12.8 %shard_map.46 = f32[16,128]{1,0:T(8,128)S(1)} custom-call(s32[1,4,16]{2,1,0:T(4,128)} %cols_in.1, s32[1,4]{1,0:T(1,128)} %counts_in.1, bf16[16,128]{1,0:T(8,128)(2,1)} %vec_in.1, bf16[1,4,16,128,128]{4,3,2,1,0:T(8,128)(2,1)} %blocks.1), custom_call_target="tpu_custom_call" | custom-call | tf_op jit(solution)/shard_map/pallas_call | solution.py:137
  12.8 0.6 %copy.6 = f32[16,128]{1,0:T(8,128)} copy(f32[16,128]{1,0:T(8,128)S(1)} %shard_map.46) | data formatting | bytes 16384

commit v5 on v4

--- a/solution.py
+++ b/solution.py
@@ -27,6 +27,13 @@
     def owner(offset):
         return (g, lax.rem(w + offset, wide))
 
+    barrier = pltpu.get_barrier_semaphore()
+    peers = [owner(d) for d in range(1, wide)]
+    for d in range(1, steps):
+        peers += [group(d), group(-d)]
+    for peer in peers:
+        pl.semaphore_signal(barrier, inc=1, device_id=peer, device_id_type=MESH)
+
     small = [
         pltpu.make_async_copy(src, dst, in_sem.at[i])
         for i, (src, dst) in enumerate(((vec_in, vec), (cols_in, cols), (counts_in, counts)))
@@ -39,12 +46,6 @@
         loads[s] = pltpu.make_async_copy(blocks.at[0, s], tiles[s], load_sem.at[s])
         loads[s].start()
 
-    barrier = pltpu.get_barrier_semaphore()
-    peers = [owner(d) for d in range(1, wide)]
-    for d in range(1, steps):
-        peers += [group(d), group(-d)]
-    for peer in peers:
-        pl.semaphore_signal(barrier, inc=1, device_id=peer, device_id_type=MESH)
     small[0].wait()
     panels[0][w] = vec[...]
     pl.semaphore_wait(barrier, len(peers))

time: 13.6 us -> 13.6 us (level)
  no operation moved by 1% of the time
where the time goes in v5:
time: 13.6 us; the launch traced here: 13.4 us
  Pallas kernels  12.8 us (94%)
  local copies, waits for them, and re-layouts  0.6 us (4%)
    pallas_call x1, Pallas kernels, shards(): pl.pallas_call(functools.partial(kernel, groups, wide, steps), out_shape=...  12.8 us
    unnamed x1, local copies, waits for them, and re-layouts  0.6 us

profile of v5, /device:TPU:0, one launch (start us, length us, event | category | flops | bytes accessed | tf_op | source)
XLA Modules:
  0.0 13.4 jit_solution(10388914160767429717)
XLA Ops:
  0.0 12.8 %shard_map.46 = f32[16,128]{1,0:T(8,128)S(1)} custom-call(s32[1,4,16]{2,1,0:T(4,128)} %cols_in.1, s32[1,4]{1,0:T(1,128)} %counts_in.1, bf16[16,128]{1,0:T(8,128)(2,1)} %vec_in.1, bf16[1,4,16,128,128]{4,3,2,1,0:T(8,128)(2,1)} %blocks.1), custom_call_target="tpu_custom_call" | custom-call | tf_op jit(solution)/shard_map/pallas_call | solution.py:138
  12.8 0.6 %copy.6 = f32[16,128]{1,0:T(8,128)} copy(f32[16,128]{1,0:T(8,128)S(1)} %shard_map.46) | data formatting | bytes 16384
